TPU v7x, 128 devices: a whole 4x4x4 slice. The times are simulated.
128 devices in a mesh: ctx: 16 (over x_lo, y, core), ch: 8 (over x_hi, z).
Axes of the slice: x: 4 (x_hi: 2, x_lo: 2; x = x_hi * 2 + x_lo), y: 4, z: 4, core: 2. Of those that a mesh axis runs over, the one named last changes fastest.
Arguments:
- query_branch: bfloat16 [4096, 8192], P('ctx', 'ch'), may hold values from -6 to 6
- key_raw: bfloat16 [4096, 8192], P('ctx', 'ch'), may hold values from -6 to 6
- value_branch: bfloat16 [4096, 8192], P('ctx', 'ch'), may hold values from -6 to 6
- conv_out: bfloat16 [4096, 8192], P('ctx', 'ch'), may hold values from -6 to 6
- out_grad: bfloat16 [4096, 8192], P('ctx', 'ch'), may hold values from -18 to 18
- long_filter: bfloat16 [4096, 8192], P('ctx', 'ch'), may hold values from -0.09375 to 0.09375
- short_filter: float32 [3, 8192], P(None, 'ch'), may hold values from -3 to 3
Outputs:
- query_grad: bfloat16 [4096, 8192], P('ctx', 'ch')
- key_raw_grad: bfloat16 [4096, 8192], P('ctx', 'ch')
- value_grad: bfloat16 [4096, 8192], P('ctx', 'ch')
- filter_grad: float32 [4096, 8192], P('ctx', 'ch')
- short_grad: float32 [3, 8192], P(None, 'ch')
All inputs are finite; a program needn't handle non-finite values.
Results may differ from a plain program's by a relative error of at most 0.0049.
Values may be sent and summed in bfloat16 or wider, within the bound.
A program may use at most 128 MiB of HBM per device.

v0:
```python
import math
import jax
import jax.numpy as jnp
from jax import lax
from jax.sharding import PartitionSpec as P

HIGHEST = lax.Precision.HIGHEST


def shifted(block, axis, distance):
    devices = range(lax.axis_size(axis))
    route = [(i - distance, i) for i in devices if i - distance in devices]
    return lax.ppermute(block, axis, route)


def spectral_tables(block_rows):
    length = 2 * block_rows
    rows_all = jnp.arange(length, dtype=jnp.int32)
    frequency = jnp.where(rows_all <= block_rows, rows_all, rows_all - block_rows)
    cosine_rows = rows_all <= block_rows
    column = jnp.arange(block_rows, dtype=jnp.int32)
    phase_index = frequency[:, None] * column[None, :] % length
    angles = phase_index.astype(jnp.float32) * (math.pi / block_rows)
    forward_table = jnp.where(cosine_rows[:, None], jnp.cos(angles), -jnp.sin(angles))
    upper = lax.optimization_barrier(forward_table.astype(jnp.bfloat16))
    lower = (forward_table - upper.astype(jnp.float32)).astype(jnp.bfloat16)
    forward_pair = jnp.concatenate([upper, lower], axis=1)
    edge = (frequency == 0) | (frequency == block_rows)
    weight = jnp.where(edge, 1.0, 2.0).astype(jnp.float32) / length
    inverse_table = forward_table.T * weight[None, :]
    parity = jnp.where(frequency % 2 == 0, 1.0, -1.0).astype(jnp.float32)[:, None]
    dc_mask = jnp.where(column == 0, 0.0, 1.0).astype(jnp.float32)[:, None]
    return (forward_pair, inverse_table, parity, dc_mask)


def forward(forward_pair, data_block):
    doubled = jnp.concatenate([data_block, data_block], axis=0)
    return jnp.dot(forward_pair, doubled, preferred_element_type=jnp.float32)


def conj_product(left, right, dc_mask):
    half = left.shape[0] // 2
    left_re, left_im = (left[:half], left[half:])
    right_re, right_im = (right[:half], right[half:])
    both_im = left_im * right_im
    real_part = left_re * right_re + dc_mask * both_im
    imag_part = dc_mask * (left_re * right_im - left_im * right_re) + (1.0 - dc_mask) * both_im
    return jnp.concatenate([real_part, imag_part], axis=0)


def sequence_blocks(long_filter, gated, conv_grad, tables):
    forward_pair, inverse_table, parity, dc_mask = tables
    block_rows, local_width = gated.shape
    block_count = lax.axis_size("ctx")
    filters = lax.all_gather(long_filter, "ctx", axis=0, tiled=True)
    gateds = lax.all_gather(gated, "ctx", axis=0, tiled=True)
    spectrum_zero = jnp.zeros((2 * block_rows, local_width), jnp.float32)

    def pair_step(turn_index, carried, grad_block):
        out_acc, lag_acc, prev_filter, prev_gated = carried
        row_start = turn_index * block_rows
        filter_block = lax.dynamic_slice_in_dim(filters, row_start, block_rows, 0)
        gated_block = lax.dynamic_slice_in_dim(gateds, row_start, block_rows, 0)
        spectra = forward(
            forward_pair, jnp.concatenate([filter_block, gated_block, grad_block], axis=1)
        )
        filter_spec = spectra[:, :local_width]
        gated_spec = spectra[:, local_width : 2 * local_width]
        grad_spec = spectra[:, 2 * local_width :]
        out_acc = out_acc + conj_product(filter_spec + parity * prev_filter, grad_spec, dc_mask)
        lag_acc = lag_acc + conj_product(gated_spec + parity * prev_gated, grad_spec, dc_mask)
        return (out_acc, lag_acc, filter_spec, gated_spec)

    initial = (spectrum_zero, spectrum_zero, spectrum_zero, spectrum_zero)

    def cycle_turn(turn_index, status):
        carried, held = status
        carried = pair_step(turn_index, carried, held)
        held = shifted(held, "ctx", -1)
        return (carried, held)

    carried, held = lax.fori_loop(0, block_count - 1, cycle_turn, (initial, conv_grad))
    carried = pair_step(block_count - 1, carried, held)
    out_acc, lag_acc = (carried[0], carried[1])
    paired = jnp.dot(
        inverse_table,
        jnp.concatenate([out_acc, lag_acc], axis=1),
        precision=HIGHEST,
        preferred_element_type=jnp.float32,
    )
    return (paired[:, :local_width], paired[:, local_width:])


def per_device(query_branch, key_raw, value_branch, conv_out, out_grad, long_filter, short_filter):
    block_rows, local_width = query_branch.shape
    tap_count = short_filter.shape[0]
    block_count = lax.axis_size("ctx")
    tables = spectral_tables(block_rows)
    before = shifted(key_raw[block_rows - (tap_count - 1) :], "ctx", 1)
    extended = jnp.concatenate([before, key_raw], axis=0).astype(jnp.float32)
    key_conv = jnp.zeros((block_rows, local_width), jnp.float32)
    for shift_tap in range(tap_count):
        key_conv = (
            key_conv
            + short_filter[shift_tap]
            * extended[tap_count - 1 - shift_tap : tap_count - 1 - shift_tap + block_rows]
        )
    value_wide = value_branch.astype(jnp.float32)
    gated = (key_conv * value_wide).astype(jnp.bfloat16)
    grad_wide = out_grad.astype(jnp.float32)
    query_grad = (grad_wide * conv_out.astype(jnp.float32)).astype(jnp.bfloat16)
    conv_grad = (grad_wide * query_branch.astype(jnp.float32)).astype(jnp.bfloat16)
    gated_grad, lag_grad = sequence_blocks(long_filter, gated, conv_grad, tables)
    value_grad = (gated_grad * key_conv).astype(jnp.bfloat16)
    key_grad = gated_grad * value_wide
    rows_next = shifted(key_grad[: tap_count - 1], "ctx", -1)
    tail_ext = jnp.concatenate([key_grad, rows_next], axis=0)
    raw_total = jnp.zeros((block_rows, local_width), jnp.float32)
    for shift_tap in range(tap_count):
        raw_total = (
            raw_total + short_filter[shift_tap] * tail_ext[shift_tap : shift_tap + block_rows]
        )
    key_raw_grad = raw_total.astype(jnp.bfloat16)
    tap_terms = jnp.stack(
        [
            jnp.sum(
                key_grad
                * extended[tap_count - 1 - shift_tap : tap_count - 1 - shift_tap + block_rows],
                axis=0,
            )
            for shift_tap in range(tap_count)
        ]
    )
    short_grad = lax.psum(tap_terms, "ctx")
    squares = jnp.sum(lag_grad * lag_grad)
    total_squares = lax.psum(squares, ("ctx", "ch"))
    entries = float(block_rows * local_width * block_count * lax.axis_size("ch"))
    scale_factor = lax.rsqrt(total_squares / entries + 1e-06)
    return (query_grad, key_raw_grad, value_grad, lag_grad * scale_factor, short_grad)


def solution(mesh):
    in_specs = (
        P("ctx", "ch"),
        P("ctx", "ch"),
        P("ctx", "ch"),
        P("ctx", "ch"),
        P("ctx", "ch"),
        P("ctx", "ch"),
        P(None, "ch"),
    )
    out_specs = (P("ctx", "ch"), P("ctx", "ch"), P("ctx", "ch"), P("ctx", "ch"), P(None, "ch"))
    return jax.shard_map(
        per_device, mesh=mesh, in_specs=in_specs, out_specs=out_specs, check_vma=False
    )
```

profile of v0, /device:TPU:0, one launch (start us, length us, event | category | flops | bytes accessed | tf_op | source)
XLA Modules:
  0.0 759.4 jit_solution(221422856139085992)
XLA Ops:
  21.9 42.5 %all-gather.3.cloned.1.call-done = bf16[4096,1024]{1,0:T(8,128)(2,1)} async-done(((bf16[256,1024]{1,0:T(8,128)(2,1)}), bf16[4096,1024]{1,0:T(8,128)(2,1)}) %all-gather.3.cloned.1.call-update) | async-done | bytes 8388624 | tf_op jit(solution)/shard_map/all_gather | solution.py:55
  66.2 53.5 %all-gather.5.cloned.1.call-done = bf16[4096,1024]{1,0:T(8,128)(2,1)} async-done(((bf16[256,1024]{1,0:T(8,128)(2,1)}), bf16[4096,1024]{1,0:T(8,128)(2,1)}) %all-gather.5.cloned.1.call-update) | async-done | bytes 8388624 | tf_op jit(solution)/shard_map/all_gather | solution.py:56
  124.7 459.0 %while.23 = (s32[]{:T(128)}, f32[512,1024]{1,0:T(8,128)}, f32[512,1024]{1,0:T(8,128)}, f32[512,1024]{1,0:T(8,128)}, f32[512,1024]{1,0:T(8,128)}, /*index=5*/bf16...) while((s32[]{:T(128)}, f32[512,1024]{1,0:T(8,128)}, ...), condition=%wide.region_1.2_spmd.clone.clone, body=%wide.region_0.1_spmd.clone.clone.sunk | while | flops 1639981824 | bytes 53486816 | solution.py:82
  130.1 12.8 %convolution_bitcast_fusion.2 = f32[512,3072]{1,0:T(8,128)S(1)} fusion(bf16[512,512]{1,0:T(8,128)(2,1)} %get-tuple-element.451, bf16[256,1024]{1,0:T(8,128)(2,1)} %copy.23, bf16[256,1024]{1,0:T(8,128)(2,1)S(1)} %constant_dynamic-slice_fusion.4, bf16[256,1024]{1,0:T(8,128)(2,1)S(1)} %constant_dynamic-slice_fusion.5), kind=kOutput, calls=%fused_computation.2.clone.1 | convolution fusion | flops 1629487104 | bytes 8388608 | tf_op jit(solution)/shard_map/while/body/eval_jaxpr/dot_general | solution.py:38
  159.5 12.8 %convolution_bitcast_fusion.2 = f32[512,3072]{1,0:T(8,128)S(1)} fusion(bf16[512,512]{1,0:T(8,128)(2,1)} %get-tuple-element.451, bf16[256,1024]{1,0:T(8,128)(2,1)} %copy.23, bf16[256,1024]{1,0:T(8,128)(2,1)S(1)} %constant_dynamic-slice_fusion.4, bf16[256,1024]{1,0:T(8,128)(2,1)S(1)} %constant_dynamic-slice_fusion.5), kind=kOutput, calls=%fused_computation.2.clone.1 | convolution fusion | flops 1629487104 | bytes 8388608 | tf_op jit(solution)/shard_map/while/body/eval_jaxpr/dot_general | solution.py:38
  179.2 5.6 maximum_add_fusion.5
  190.2 12.8 %convolution_bitcast_fusion.2 = f32[512,3072]{1,0:T(8,128)S(1)} fusion(bf16[512,512]{1,0:T(8,128)(2,1)} %get-tuple-element.451, bf16[256,1024]{1,0:T(8,128)(2,1)} %copy.23, bf16[256,1024]{1,0:T(8,128)(2,1)S(1)} %constant_dynamic-slice_fusion.4, bf16[256,1024]{1,0:T(8,128)(2,1)S(1)} %constant_dynamic-slice_fusion.5), kind=kOutput, calls=%fused_computation.2.clone.1 | convolution fusion | flops 1629487104 | bytes 8388608 | tf_op jit(solution)/shard_map/while/body/eval_jaxpr/dot_general | solution.py:38
  209.9 5.6 maximum_add_fusion.5
  220.9 12.8 %convolution_bitcast_fusion.2 = f32[512,3072]{1,0:T(8,128)S(1)} fusion(bf16[512,512]{1,0:T(8,128)(2,1)} %get-tuple-element.451, bf16[256,1024]{1,0:T(8,128)(2,1)} %copy.23, bf16[256,1024]{1,0:T(8,128)(2,1)S(1)} %constant_dynamic-slice_fusion.4, bf16[256,1024]{1,0:T(8,128)(2,1)S(1)} %constant_dynamic-slice_fusion.5), kind=kOutput, calls=%fused_computation.2.clone.1 | convolution fusion | flops 1629487104 | bytes 8388608 | tf_op jit(solution)/shard_map/while/body/eval_jaxpr/dot_general | solution.py:38
  240.6 5.6 maximum_add_fusion.5
  251.6 12.8 %convolution_bitcast_fusion.2 = f32[512,3072]{1,0:T(8,128)S(1)} fusion(bf16[512,512]{1,0:T(8,128)(2,1)} %get-tuple-element.451, bf16[256,1024]{1,0:T(8,128)(2,1)} %copy.23, bf16[256,1024]{1,0:T(8,128)(2,1)S(1)} %constant_dynamic-slice_fusion.4, bf16[256,1024]{1,0:T(8,128)(2,1)S(1)} %constant_dynamic-slice_fusion.5), kind=kOutput, calls=%fused_computation.2.clone.1 | convolution fusion | flops 1629487104 | bytes 8388608 | tf_op jit(solution)/shard_map/while/body/eval_jaxpr/dot_general | solution.py:38
  271.3 5.6 maximum_add_fusion.5
  282.2 12.8 %convolution_bitcast_fusion.2 = f32[512,3072]{1,0:T(8,128)S(1)} fusion(bf16[512,512]{1,0:T(8,128)(2,1)} %get-tuple-element.451, bf16[256,1024]{1,0:T(8,128)(2,1)} %copy.23, bf16[256,1024]{1,0:T(8,128)(2,1)S(1)} %constant_dynamic-slice_fusion.4, bf16[256,1024]{1,0:T(8,128)(2,1)S(1)} %constant_dynamic-slice_fusion.5), kind=kOutput, calls=%fused_computation.2.clone.1 | convolution fusion | flops 1629487104 | bytes 8388608 | tf_op jit(solution)/shard_map/while/body/eval_jaxpr/dot_general | solution.py:38
  302.0 5.6 maximum_add_fusion.5
  312.9 12.8 %convolution_bitcast_fusion.2 = f32[512,3072]{1,0:T(8,128)S(1)} fusion(bf16[512,512]{1,0:T(8,128)(2,1)} %get-tuple-element.451, bf16[256,1024]{1,0:T(8,128)(2,1)} %copy.23, bf16[256,1024]{1,0:T(8,128)(2,1)S(1)} %constant_dynamic-slice_fusion.4, bf16[256,1024]{1,0:T(8,128)(2,1)S(1)} %constant_dynamic-slice_fusion.5), kind=kOutput, calls=%fused_computation.2.clone.1 | convolution fusion | flops 1629487104 | bytes 8388608 | tf_op jit(solution)/shard_map/while/body/eval_jaxpr/dot_general | solution.py:38
  332.7 5.6 maximum_add_fusion.5
  343.6 12.8 %convolution_bitcast_fusion.2 = f32[512,3072]{1,0:T(8,128)S(1)} fusion(bf16[512,512]{1,0:T(8,128)(2,1)} %get-tuple-element.451, bf16[256,1024]{1,0:T(8,128)(2,1)} %copy.23, bf16[256,1024]{1,0:T(8,128)(2,1)S(1)} %constant_dynamic-slice_fusion.4, bf16[256,1024]{1,0:T(8,128)(2,1)S(1)} %constant_dynamic-slice_fusion.5), kind=kOutput, calls=%fused_computation.2.clone.1 | convolution fusion | flops 1629487104 | bytes 8388608 | tf_op jit(solution)/shard_map/while/body/eval_jaxpr/dot_general | solution.py:38
  363.4 5.6 maximum_add_fusion.5
  374.3 12.8 %convolution_bitcast_fusion.2 = f32[512,3072]{1,0:T(8,128)S(1)} fusion(bf16[512,512]{1,0:T(8,128)(2,1)} %get-tuple-element.451, bf16[256,1024]{1,0:T(8,128)(2,1)} %copy.23, bf16[256,1024]{1,0:T(8,128)(2,1)S(1)} %constant_dynamic-slice_fusion.4, bf16[256,1024]{1,0:T(8,128)(2,1)S(1)} %constant_dynamic-slice_fusion.5), kind=kOutput, calls=%fused_computation.2.clone.1 | convolution fusion | flops 1629487104 | bytes 8388608 | tf_op jit(solution)/shard_map/while/body/eval_jaxpr/dot_general | solution.py:38
  394.1 5.6 maximum_add_fusion.5
  405.0 12.8 %convolution_bitcast_fusion.2 = f32[512,3072]{1,0:T(8,128)S(1)} fusion(bf16[512,512]{1,0:T(8,128)(2,1)} %get-tuple-element.451, bf16[256,1024]{1,0:T(8,128)(2,1)} %copy.23, bf16[256,1024]{1,0:T(8,128)(2,1)S(1)} %constant_dynamic-slice_fusion.4, bf16[256,1024]{1,0:T(8,128)(2,1)S(1)} %constant_dynamic-slice_fusion.5), kind=kOutput, calls=%fused_computation.2.clone.1 | convolution fusion | flops 1629487104 | bytes 8388608 | tf_op jit(solution)/shard_map/while/body/eval_jaxpr/dot_general | solution.py:38
  435.7 12.8 %convolution_bitcast_fusion.2 = f32[512,3072]{1,0:T(8,128)S(1)} fusion(bf16[512,512]{1,0:T(8,128)(2,1)} %get-tuple-element.451, bf16[256,1024]{1,0:T(8,128)(2,1)} %copy.23, bf16[256,1024]{1,0:T(8,128)(2,1)S(1)} %constant_dynamic-slice_fusion.4, bf16[256,1024]{1,0:T(8,128)(2,1)S(1)} %constant_dynamic-slice_fusion.5), kind=kOutput, calls=%fused_computation.2.clone.1 | convolution fusion | flops 1629487104 | bytes 8388608 | tf_op jit(solution)/shard_map/while/body/eval_jaxpr/dot_general | solution.py:38
  466.4 12.8 %convolution_bitcast_fusion.2 = f32[512,3072]{1,0:T(8,128)S(1)} fusion(bf16[512,512]{1,0:T(8,128)(2,1)} %get-tuple-element.451, bf16[256,1024]{1,0:T(8,128)(2,1)} %copy.23, bf16[256,1024]{1,0:T(8,128)(2,1)S(1)} %constant_dynamic-slice_fusion.4, bf16[256,1024]{1,0:T(8,128)(2,1)S(1)} %constant_dynamic-slice_fusion.5), kind=kOutput, calls=%fused_computation.2.clone.1 | convolution fusion | flops 1629487104 | bytes 8388608 | tf_op jit(solution)/shard_map/while/body/eval_jaxpr/dot_general | solution.py:38
  497.1 12.8 %convolution_bitcast_fusion.2 = f32[512,3072]{1,0:T(8,128)S(1)} fusion(bf16[512,512]{1,0:T(8,128)(2,1)} %get-tuple-element.451, bf16[256,1024]{1,0:T(8,128)(2,1)} %copy.23, bf16[256,1024]{1,0:T(8,128)(2,1)S(1)} %constant_dynamic-slice_fusion.4, bf16[256,1024]{1,0:T(8,128)(2,1)S(1)} %constant_dynamic-slice_fusion.5), kind=kOutput, calls=%fused_computation.2.clone.1 | convolution fusion | flops 1629487104 | bytes 8388608 | tf_op jit(solution)/shard_map/while/body/eval_jaxpr/dot_general | solution.py:38
  527.8 12.8 %convolution_bitcast_fusion.2 = f32[512,3072]{1,0:T(8,128)S(1)} fusion(bf16[512,512]{1,0:T(8,128)(2,1)} %get-tuple-element.451, bf16[256,1024]{1,0:T(8,128)(2,1)} %copy.23, bf16[256,1024]{1,0:T(8,128)(2,1)S(1)} %constant_dynamic-slice_fusion.4, bf16[256,1024]{1,0:T(8,128)(2,1)S(1)} %constant_dynamic-slice_fusion.5), kind=kOutput, calls=%fused_computation.2.clone.1 | convolution fusion | flops 1629487104 | bytes 8388608 | tf_op jit(solution)/shard_map/while/body/eval_jaxpr/dot_general | solution.py:38
  547.5 5.6 maximum_add_fusion.5
  558.5 12.8 %convolution_bitcast_fusion.2 = f32[512,3072]{1,0:T(8,128)S(1)} fusion(bf16[512,512]{1,0:T(8,128)(2,1)} %get-tuple-element.451, bf16[256,1024]{1,0:T(8,128)(2,1)} %copy.23, bf16[256,1024]{1,0:T(8,128)(2,1)S(1)} %constant_dynamic-slice_fusion.4, bf16[256,1024]{1,0:T(8,128)(2,1)S(1)} %constant_dynamic-slice_fusion.5), kind=kOutput, calls=%fused_computation.2.clone.1 | convolution fusion | flops 1629487104 | bytes 8388608 | tf_op jit(solution)/shard_map/while/body/eval_jaxpr/dot_general | solution.py:38
  578.2 5.6 maximum_add_fusion.5
  583.8 6.4 fusion.21
  596.5 5.8 fusion.17
  603.1 85.2 %psum.14 = f32[]{:T(128)} all-reduce(f32[]{:T(128)} %multiply_reduce_fusion.3), channel_id=1, replica_groups=mesh['ctx'=16,'ch'=8] {'ctx','ch'}, use_global_device_ids=true, to_apply=%region_3.4 | all-reduce | flops 1 | bytes 8 | tf_op jit(solution)/shard_map/psum | solution.py:136
  694.4 55.0 %psum.15 = f32[3,1024]{1,0:T(4,128)} all-reduce(f32[3,1024]{1,0:T(4,128)S(1)} %pad_maximum_fusion.2), channel_id=1, replica_groups=mesh['ctx'=16,'ch'=8] {'ctx'}, use_global_device_ids=true, to_apply=%region_7.8 | all-reduce | flops 3072 | bytes 24576 | tf_op jit(solution)/shard_map/psum | solution.py:134
  (211 shorter events, 248.1 us)
Async XLA Ops:
  7.2 4.9 copy-start.5
  7.2 57.1 %all-gather.3.cloned.1.call-start = ((), (), s32[]{:S(2)}) async-start(), calls=%async_computation | async-start | bytes 8912896 | tf_op jit(solution)/shard_map/all_gather | solution.py:55
  7.9 111.8 %all-gather.5.cloned.1.call-start = ((), (), s32[]{:S(2)}) async-start(), calls=%async_computation.1 | async-start | bytes 8912896 | tf_op jit(solution)/shard_map/all_gather | solution.py:56
  8.7 2.1 collective-permute-start.1
  12.0 1.6 copy-start.2
  13.6 7.0 copy-start.7
  13.6 7.0 copy-start.8
  13.6 7.0 copy-start.9
  19.0 0.7 copy-start.6
  126.6 27.5 %collective-permute-start = (bf16[256,1024]{1,0:T(8,128)(2,1)}, bf16[256,1024]{1,0:T(8,128)(2,1)}, u32[]{:S(2)}, u32[]{:S(2)}) collective-permute-start(bf16[256,1024]{1,0:T(8,128)(2,1)} %copy.23), channel_id=1, source_target_pairs={{8,0},{16,8},{24,16},{32,24},{40,32},{48,40},{56,48},{64,56},{72,6... | collective-permute-start | bytes 1572872 | tf_op jit(solution)/shard_map/while/body/eval_jaxpr/ppermute | solution.py:13
  156.0 28.8 %collective-permute-start = (bf16[256,1024]{1,0:T(8,128)(2,1)}, bf16[256,1024]{1,0:T(8,128)(2,1)}, u32[]{:S(2)}, u32[]{:S(2)}) collective-permute-start(bf16[256,1024]{1,0:T(8,128)(2,1)} %copy.23), channel_id=1, source_target_pairs={{8,0},{16,8},{24,16},{32,24},{40,32},{48,40},{56,48},{64,56},{72,6... | collective-permute-start | bytes 1572872 | tf_op jit(solution)/shard_map/while/body/eval_jaxpr/ppermute | solution.py:13
  186.7 28.8 %collective-permute-start = (bf16[256,1024]{1,0:T(8,128)(2,1)}, bf16[256,1024]{1,0:T(8,128)(2,1)}, u32[]{:S(2)}, u32[]{:S(2)}) collective-permute-start(bf16[256,1024]{1,0:T(8,128)(2,1)} %copy.23), channel_id=1, source_target_pairs={{8,0},{16,8},{24,16},{32,24},{40,32},{48,40},{56,48},{64,56},{72,6... | collective-permute-start | bytes 1572872 | tf_op jit(solution)/shard_map/while/body/eval_jaxpr/ppermute | solution.py:13
  217.4 28.8 %collective-permute-start = (bf16[256,1024]{1,0:T(8,128)(2,1)}, bf16[256,1024]{1,0:T(8,128)(2,1)}, u32[]{:S(2)}, u32[]{:S(2)}) collective-permute-start(bf16[256,1024]{1,0:T(8,128)(2,1)} %copy.23), channel_id=1, source_target_pairs={{8,0},{16,8},{24,16},{32,24},{40,32},{48,40},{56,48},{64,56},{72,6... | collective-permute-start | bytes 1572872 | tf_op jit(solution)/shard_map/while/body/eval_jaxpr/ppermute | solution.py:13
  248.0 28.8 %collective-permute-start = (bf16[256,1024]{1,0:T(8,128)(2,1)}, bf16[256,1024]{1,0:T(8,128)(2,1)}, u32[]{:S(2)}, u32[]{:S(2)}) collective-permute-start(bf16[256,1024]{1,0:T(8,128)(2,1)} %copy.23), channel_id=1, source_target_pairs={{8,0},{16,8},{24,16},{32,24},{40,32},{48,40},{56,48},{64,56},{72,6... | collective-permute-start | bytes 1572872 | tf_op jit(solution)/shard_map/while/body/eval_jaxpr/ppermute | solution.py:13
  278.7 28.8 %collective-permute-start = (bf16[256,1024]{1,0:T(8,128)(2,1)}, bf16[256,1024]{1,0:T(8,128)(2,1)}, u32[]{:S(2)}, u32[]{:S(2)}) collective-permute-start(bf16[256,1024]{1,0:T(8,128)(2,1)} %copy.23), channel_id=1, source_target_pairs={{8,0},{16,8},{24,16},{32,24},{40,32},{48,40},{56,48},{64,56},{72,6... | collective-permute-start | bytes 1572872 | tf_op jit(solution)/shard_map/while/body/eval_jaxpr/ppermute | solution.py:13
  309.4 28.8 %collective-permute-start = (bf16[256,1024]{1,0:T(8,128)(2,1)}, bf16[256,1024]{1,0:T(8,128)(2,1)}, u32[]{:S(2)}, u32[]{:S(2)}) collective-permute-start(bf16[256,1024]{1,0:T(8,128)(2,1)} %copy.23), channel_id=1, source_target_pairs={{8,0},{16,8},{24,16},{32,24},{40,32},{48,40},{56,48},{64,56},{72,6... | collective-permute-start | bytes 1572872 | tf_op jit(solution)/shard_map/while/body/eval_jaxpr/ppermute | solution.py:13
  340.1 28.8 %collective-permute-start = (bf16[256,1024]{1,0:T(8,128)(2,1)}, bf16[256,1024]{1,0:T(8,128)(2,1)}, u32[]{:S(2)}, u32[]{:S(2)}) collective-permute-start(bf16[256,1024]{1,0:T(8,128)(2,1)} %copy.23), channel_id=1, source_target_pairs={{8,0},{16,8},{24,16},{32,24},{40,32},{48,40},{56,48},{64,56},{72,6... | collective-permute-start | bytes 1572872 | tf_op jit(solution)/shard_map/while/body/eval_jaxpr/ppermute | solution.py:13
  370.8 28.8 %collective-permute-start = (bf16[256,1024]{1,0:T(8,128)(2,1)}, bf16[256,1024]{1,0:T(8,128)(2,1)}, u32[]{:S(2)}, u32[]{:S(2)}) collective-permute-start(bf16[256,1024]{1,0:T(8,128)(2,1)} %copy.23), channel_id=1, source_target_pairs={{8,0},{16,8},{24,16},{32,24},{40,32},{48,40},{56,48},{64,56},{72,6... | collective-permute-start | bytes 1572872 | tf_op jit(solution)/shard_map/while/body/eval_jaxpr/ppermute | solution.py:13
  401.5 28.8 %collective-permute-start = (bf16[256,1024]{1,0:T(8,128)(2,1)}, bf16[256,1024]{1,0:T(8,128)(2,1)}, u32[]{:S(2)}, u32[]{:S(2)}) collective-permute-start(bf16[256,1024]{1,0:T(8,128)(2,1)} %copy.23), channel_id=1, source_target_pairs={{8,0},{16,8},{24,16},{32,24},{40,32},{48,40},{56,48},{64,56},{72,6... | collective-permute-start | bytes 1572872 | tf_op jit(solution)/shard_map/while/body/eval_jaxpr/ppermute | solution.py:13
  432.2 28.8 %collective-permute-start = (bf16[256,1024]{1,0:T(8,128)(2,1)}, bf16[256,1024]{1,0:T(8,128)(2,1)}, u32[]{:S(2)}, u32[]{:S(2)}) collective-permute-start(bf16[256,1024]{1,0:T(8,128)(2,1)} %copy.23), channel_id=1, source_target_pairs={{8,0},{16,8},{24,16},{32,24},{40,32},{48,40},{56,48},{64,56},{72,6... | collective-permute-start | bytes 1572872 | tf_op jit(solution)/shard_map/while/body/eval_jaxpr/ppermute | solution.py:13
  462.9 28.8 %collective-permute-start = (bf16[256,1024]{1,0:T(8,128)(2,1)}, bf16[256,1024]{1,0:T(8,128)(2,1)}, u32[]{:S(2)}, u32[]{:S(2)}) collective-permute-start(bf16[256,1024]{1,0:T(8,128)(2,1)} %copy.23), channel_id=1, source_target_pairs={{8,0},{16,8},{24,16},{32,24},{40,32},{48,40},{56,48},{64,56},{72,6... | collective-permute-start | bytes 1572872 | tf_op jit(solution)/shard_map/while/body/eval_jaxpr/ppermute | solution.py:13
  493.6 28.8 %collective-permute-start = (bf16[256,1024]{1,0:T(8,128)(2,1)}, bf16[256,1024]{1,0:T(8,128)(2,1)}, u32[]{:S(2)}, u32[]{:S(2)}) collective-permute-start(bf16[256,1024]{1,0:T(8,128)(2,1)} %copy.23), channel_id=1, source_target_pairs={{8,0},{16,8},{24,16},{32,24},{40,32},{48,40},{56,48},{64,56},{72,6... | collective-permute-start | bytes 1572872 | tf_op jit(solution)/shard_map/while/body/eval_jaxpr/ppermute | solution.py:13
  524.3 28.8 %collective-permute-start = (bf16[256,1024]{1,0:T(8,128)(2,1)}, bf16[256,1024]{1,0:T(8,128)(2,1)}, u32[]{:S(2)}, u32[]{:S(2)}) collective-permute-start(bf16[256,1024]{1,0:T(8,128)(2,1)} %copy.23), channel_id=1, source_target_pairs={{8,0},{16,8},{24,16},{32,24},{40,32},{48,40},{56,48},{64,56},{72,6... | collective-permute-start | bytes 1572872 | tf_op jit(solution)/shard_map/while/body/eval_jaxpr/ppermute | solution.py:13
  555.0 28.8 %collective-permute-start = (bf16[256,1024]{1,0:T(8,128)(2,1)}, bf16[256,1024]{1,0:T(8,128)(2,1)}, u32[]{:S(2)}, u32[]{:S(2)}) collective-permute-start(bf16[256,1024]{1,0:T(8,128)(2,1)} %copy.23), channel_id=1, source_target_pairs={{8,0},{16,8},{24,16},{32,24},{40,32},{48,40},{56,48},{64,56},{72,6... | collective-permute-start | bytes 1572872 | tf_op jit(solution)/shard_map/while/body/eval_jaxpr/ppermute | solution.py:13
  592.9 1.6 copy-start
  592.9 2.2 copy-start.1
  596.4 92.6 %copy-start.3 = (f32[258,1024]{1,0:T(8,128)S(1)}, f32[258,1024]{1,0:T(8,128)}, u32[]{:S(2)}) copy-start(f32[258,1024]{1,0:T(8,128)} %copy-done.2) | copy-start | bytes 3170308
  692.1 1.0 copy-start.4
  693.1 56.3 %collective-permute-start.2 = (f32[2,1024]{1,0:T(2,128)S(1)}, f32[2,1024]{1,0:T(2,128)S(1)}, u32[]{:S(2)}, u32[]{:S(2)}) collective-permute-start(f32[2,1024]{1,0:T(2,128)S(1)} %slice.190), channel_id=1, source_target_pairs={{8,0},{16,8},{24,16},{32,24},{40,32},{48,40},{56,48},{64,56},{72,6... | collective-permute-start | bytes 24584 | tf_op jit(solution)/shard_map/ppermute | solution.py:13
Sparse Core Ops, SparseCore 0:
  9.7 54.5 all-gather.2
  66.6 53.0 all-gather.4
where the time goes:
time: 763 us; the launch traced here: 759 us
  other arithmetic  209 us (27%)
  matrix products  204 us (27%)
  blocking collectives  140 us (18%)
  waiting for transfers between devices  96.7 us (13%)
  local copies, waits for them, and re-layouts  71.7 us (9%)
  starting transfers between devices  21.8 us (3%)
  between operations  15 us (2%)
    dot_general x16, matrix products, forward(): return jnp.dot(forward_pair, doubled, preferred_element_type=jnp.float32)  198 us
    psum x1, blocking collectives, per_device(): total_squares = lax.psum(squares, ('ctx', 'ch'))  85.2 us
    add x16, other arithmetic, pair_step(): out_acc + conj_product(filter_spec + parity * prev_filter, grad_spec, dc_...  83.3 us
    add x15, other arithmetic, pair_step(): gated_spec + parity * prev_gated  75.7 us
    psum x1, blocking collectives, per_device(): short_grad = lax.psum(tap_terms, 'ctx')  55 us
    all_gather x1, waiting for transfers between devices, sequence_blocks(): gateds = lax.all_gather(gated, 'ctx', axis=0, tiled=True)  53.5 us
    all_gather x1, waiting for transfers between devices, sequence_blocks(): filters = lax.all_gather(long_filter, 'ctx', axis=0, tiled=True)  42.5 us
    add x16, other arithmetic, conj_product(): real_part = left_re * right_re + dc_mask * both_im  29.9 us
  transfers between devices with their start and end apart: 19, of which 2 were waited for; matrix products, arithmetic and copies ran while one was open for 56% of the time, Pallas kernels for 0%

commit v1 on v0

--- a/solution.py
+++ b/solution.py
@@ -5,6 +5,13 @@
 from jax.sharding import PartitionSpec as P
 
 HIGHEST = lax.Precision.HIGHEST
+
+
+def exchange_gather(block, mesh_axis, dim):
+    devices = lax.axis_size(mesh_axis)
+    shards = jnp.stack([block for _ in range(devices)])
+    shards = lax.all_to_all(shards, mesh_axis, split_axis=0, concat_axis=0)
+    return jnp.concatenate(shards, axis=dim)
 
 
 def shifted(block, axis, distance):
@@ -52,7 +59,7 @@
     forward_pair, inverse_table, parity, dc_mask = tables
     block_rows, local_width = gated.shape
     block_count = lax.axis_size("ctx")
-    filters = lax.all_gather(long_filter, "ctx", axis=0, tiled=True)
+    filters = exchange_gather(long_filter, "ctx", 0)
     gateds = lax.all_gather(gated, "ctx", axis=0, tiled=True)
     spectrum_zero = jnp.zeros((2 * block_rows, local_width), jnp.float32)
 

time: 763 us -> 820 us (1.075)
  waiting for transfers between devices: 96.7 us -> 139 us
  starting transfers between devices: 21.8 us -> 30.2 us
    all_to_all x0 -> x1, waiting for transfers between devices: none -> 139 us  [exchange_gather(): shards = lax.all_to_all(shards, mesh_axis, split_axis=0, concat_axis=0)]
    all_gather x1, waiting for transfers between devices: 53.5 us -> 0.01 us  [sequence_blocks(): gateds = lax.all_gather(gated, 'ctx', axis=0, tiled=True)]
    all_gather x1 -> x0, waiting for transfers between devices: 42.5 us -> none  [sequence_blocks(): filters = lax.all_gather(long_filter, 'ctx', axis=0, tiled=True)]
    all_to_all x0 -> x1, starting transfers between devices: none -> 8.4 us  [exchange_gather(): shards = lax.all_to_all(shards, mesh_axis, split_axis=0, concat_axis=0)]
  transfers between devices with their start and end apart: 19 -> 19, of which waited for: 2 -> 1; matrix products, arithmetic and copies ran while one was open for 56% -> 52% of each run, Pallas kernels for 0% -> 0%
where the time goes in v1:
time: 820 us; the launch traced here: 816 us
  other arithmetic  210 us (26%)
  matrix products  204 us (25%)
  blocking collectives  141 us (17%)
  waiting for transfers between devices  139 us (17%)
  local copies, waits for them, and re-layouts  76 us (9%)
  starting transfers between devices  30.2 us (4%)
  between operations  15 us (2%)
    dot_general x16, matrix products, forward(): return jnp.dot(forward_pair, doubled, preferred_element_type=jnp.float32)  198 us
    all_to_all x1, waiting for transfers between devices, exchange_gather(): shards = lax.all_to_all(shards, mesh_axis, split_axis=0, concat_axis=0)  139 us
    psum x1, blocking collectives, per_device(): total_squares = lax.psum(squares, ('ctx', 'ch'))  85.7 us
    add x16, other arithmetic, pair_step(): out_acc + conj_product(filter_spec + parity * prev_filter, grad_spec, dc_...  83.6 us
    add x15, other arithmetic, pair_step(): gated_spec + parity * prev_gated  74.9 us
    psum x1, blocking collectives, per_device(): short_grad = lax.psum(tap_terms, 'ctx')  54.9 us
    add x16, other arithmetic, conj_product(): real_part = left_re * right_re + dc_mask * both_im  30 us
    while x15, local copies, waits for them, and re-layouts  27.9 us
  transfers between devices with their start and end apart: 19, of which 1 were waited for; matrix products, arithmetic and copies ran while one was open for 52% of the time, Pallas kernels for 0%

profile of v1, /device:TPU:0, one launch (start us, length us, event | category | flops | bytes accessed | tf_op | source)
XLA Modules:
  0.0 815.9 jit_solution(14653266721388727177)
XLA Ops:
  18.6 8.4 %all-to-all-start = ((bf16[16,256,1024]{2,1,0:T(8,128)(2,1)}), bf16[16,256,1024]{2,1,0:T(8,128)(2,1)}, u32[]{:S(2)}, u32[]{:S(2)}) async-start(bf16[16,256,1024]{2,1,0:T(8,128)(2,1)} %stack.10), calls=%async_computation | async-start | bytes 16777216 | tf_op jit(solution)/shard_map/all_to_all | solution.py:13
  35.3 139.2 %all-to-all-done = bf16[16,256,1024]{2,1,0:T(8,128)(2,1)} async-done(((bf16[16,256,1024]{2,1,0:T(8,128)(2,1)}), bf16[16,256,1024]{2,1,0:T(8,128)(2,1)}, u32[]{:S(2)}, u32[]{:S(2)}) %all-to-all-start) | async-done | bytes 8388640 | tf_op jit(solution)/shard_map/all_to_all | solution.py:13
  181.5 458.5 %while.23 = (s32[]{:T(128)}, f32[512,1024]{1,0:T(8,128)}, f32[512,1024]{1,0:T(8,128)}, f32[512,1024]{1,0:T(8,128)}, f32[512,1024]{1,0:T(8,128)}, /*index=5*/bf16...) while((s32[]{:T(128)}, f32[512,1024]{1,0:T(8,128)}, ...), condition=%wide.region_1.2_spmd.clone.clone, body=%wide.region_0.1_spmd.clone.clone.sunk | while | flops 1639981824 | bytes 53486816 | solution.py:89
  186.8 12.8 %convolution_bitcast_fusion.2 = f32[512,3072]{1,0:T(8,128)S(1)} fusion(bf16[512,512]{1,0:T(8,128)(2,1)} %get-tuple-element.451, bf16[256,1024]{1,0:T(8,128)(2,1)} %copy.23, bf16[256,1024]{1,0:T(8,128)(2,1)S(1)} %constant_dynamic-slice_fusion.4, bf16[256,1024]{1,0:T(8,128)(2,1)S(1)} %constant_dynamic-slice_fusion.5), kind=kOutput, calls=%fused_computation.2.clone.1 | convolution fusion | flops 1629487104 | bytes 8388608 | tf_op jit(solution)/shard_map/while/body/eval_jaxpr/dot_general | solution.py:45
  216.2 12.8 %convolution_bitcast_fusion.2 = f32[512,3072]{1,0:T(8,128)S(1)} fusion(bf16[512,512]{1,0:T(8,128)(2,1)} %get-tuple-element.451, bf16[256,1024]{1,0:T(8,128)(2,1)} %copy.23, bf16[256,1024]{1,0:T(8,128)(2,1)S(1)} %constant_dynamic-slice_fusion.4, bf16[256,1024]{1,0:T(8,128)(2,1)S(1)} %constant_dynamic-slice_fusion.5), kind=kOutput, calls=%fused_computation.2.clone.1 | convolution fusion | flops 1629487104 | bytes 8388608 | tf_op jit(solution)/shard_map/while/body/eval_jaxpr/dot_general | solution.py:45
  235.9 5.6 maximum_add_fusion.5
  246.8 12.8 %convolution_bitcast_fusion.2 = f32[512,3072]{1,0:T(8,128)S(1)} fusion(bf16[512,512]{1,0:T(8,128)(2,1)} %get-tuple-element.451, bf16[256,1024]{1,0:T(8,128)(2,1)} %copy.23, bf16[256,1024]{1,0:T(8,128)(2,1)S(1)} %constant_dynamic-slice_fusion.4, bf16[256,1024]{1,0:T(8,128)(2,1)S(1)} %constant_dynamic-slice_fusion.5), kind=kOutput, calls=%fused_computation.2.clone.1 | convolution fusion | flops 1629487104 | bytes 8388608 | tf_op jit(solution)/shard_map/while/body/eval_jaxpr/dot_general | solution.py:45
  277.5 12.8 %convolution_bitcast_fusion.2 = f32[512,3072]{1,0:T(8,128)S(1)} fusion(bf16[512,512]{1,0:T(8,128)(2,1)} %get-tuple-element.451, bf16[256,1024]{1,0:T(8,128)(2,1)} %copy.23, bf16[256,1024]{1,0:T(8,128)(2,1)S(1)} %constant_dynamic-slice_fusion.4, bf16[256,1024]{1,0:T(8,128)(2,1)S(1)} %constant_dynamic-slice_fusion.5), kind=kOutput, calls=%fused_computation.2.clone.1 | convolution fusion | flops 1629487104 | bytes 8388608 | tf_op jit(solution)/shard_map/while/body/eval_jaxpr/dot_general | solution.py:45
  297.2 5.6 maximum_add_fusion.5
  308.1 12.8 %convolution_bitcast_fusion.2 = f32[512,3072]{1,0:T(8,128)S(1)} fusion(bf16[512,512]{1,0:T(8,128)(2,1)} %get-tuple-element.451, bf16[256,1024]{1,0:T(8,128)(2,1)} %copy.23, bf16[256,1024]{1,0:T(8,128)(2,1)S(1)} %constant_dynamic-slice_fusion.4, bf16[256,1024]{1,0:T(8,128)(2,1)S(1)} %constant_dynamic-slice_fusion.5), kind=kOutput, calls=%fused_computation.2.clone.1 | convolution fusion | flops 1629487104 | bytes 8388608 | tf_op jit(solution)/shard_map/while/body/eval_jaxpr/dot_general | solution.py:45
  327.8 5.6 maximum_add_fusion.5
  338.8 12.8 %convolution_bitcast_fusion.2 = f32[512,3072]{1,0:T(8,128)S(1)} fusion(bf16[512,512]{1,0:T(8,128)(2,1)} %get-tuple-element.451, bf16[256,1024]{1,0:T(8,128)(2,1)} %copy.23, bf16[256,1024]{1,0:T(8,128)(2,1)S(1)} %constant_dynamic-slice_fusion.4, bf16[256,1024]{1,0:T(8,128)(2,1)S(1)} %constant_dynamic-slice_fusion.5), kind=kOutput, calls=%fused_computation.2.clone.1 | convolution fusion | flops 1629487104 | bytes 8388608 | tf_op jit(solution)/shard_map/while/body/eval_jaxpr/dot_general | solution.py:45
  358.5 5.6 maximum_add_fusion.5
  369.4 12.8 %convolution_bitcast_fusion.2 = f32[512,3072]{1,0:T(8,128)S(1)} fusion(bf16[512,512]{1,0:T(8,128)(2,1)} %get-tuple-element.451, bf16[256,1024]{1,0:T(8,128)(2,1)} %copy.23, bf16[256,1024]{1,0:T(8,128)(2,1)S(1)} %constant_dynamic-slice_fusion.4, bf16[256,1024]{1,0:T(8,128)(2,1)S(1)} %constant_dynamic-slice_fusion.5), kind=kOutput, calls=%fused_computation.2.clone.1 | convolution fusion | flops 1629487104 | bytes 8388608 | tf_op jit(solution)/shard_map/while/body/eval_jaxpr/dot_general | solution.py:45
  389.2 5.6 maximum_add_fusion.5
  400.1 12.8 %convolution_bitcast_fusion.2 = f32[512,3072]{1,0:T(8,128)S(1)} fusion(bf16[512,512]{1,0:T(8,128)(2,1)} %get-tuple-element.451, bf16[256,1024]{1,0:T(8,128)(2,1)} %copy.23, bf16[256,1024]{1,0:T(8,128)(2,1)S(1)} %constant_dynamic-slice_fusion.4, bf16[256,1024]{1,0:T(8,128)(2,1)S(1)} %constant_dynamic-slice_fusion.5), kind=kOutput, calls=%fused_computation.2.clone.1 | convolution fusion | flops 1629487104 | bytes 8388608 | tf_op jit(solution)/shard_map/while/body/eval_jaxpr/dot_general | solution.py:45
  419.8 5.6 maximum_add_fusion.5
  430.8 12.8 %convolution_bitcast_fusion.2 = f32[512,3072]{1,0:T(8,128)S(1)} fusion(bf16[512,512]{1,0:T(8,128)(2,1)} %get-tuple-element.451, bf16[256,1024]{1,0:T(8,128)(2,1)} %copy.23, bf16[256,1024]{1,0:T(8,128)(2,1)S(1)} %constant_dynamic-slice_fusion.4, bf16[256,1024]{1,0:T(8,128)(2,1)S(1)} %constant_dynamic-slice_fusion.5), kind=kOutput, calls=%fused_computation.2.clone.1 | convolution fusion | flops 1629487104 | bytes 8388608 | tf_op jit(solution)/shard_map/while/body/eval_jaxpr/dot_general | solution.py:45
  450.5 5.6 maximum_add_fusion.5
  461.4 12.8 %convolution_bitcast_fusion.2 = f32[512,3072]{1,0:T(8,128)S(1)} fusion(bf16[512,512]{1,0:T(8,128)(2,1)} %get-tuple-element.451, bf16[256,1024]{1,0:T(8,128)(2,1)} %copy.23, bf16[256,1024]{1,0:T(8,128)(2,1)S(1)} %constant_dynamic-slice_fusion.4, bf16[256,1024]{1,0:T(8,128)(2,1)S(1)} %constant_dynamic-slice_fusion.5), kind=kOutput, calls=%fused_computation.2.clone.1 | convolution fusion | flops 1629487104 | bytes 8388608 | tf_op jit(solution)/shard_map/while/body/eval_jaxpr/dot_general | solution.py:45
  481.1 5.6 maximum_add_fusion.5
  492.1 12.8 %convolution_bitcast_fusion.2 = f32[512,3072]{1,0:T(8,128)S(1)} fusion(bf16[512,512]{1,0:T(8,128)(2,1)} %get-tuple-element.451, bf16[256,1024]{1,0:T(8,128)(2,1)} %copy.23, bf16[256,1024]{1,0:T(8,128)(2,1)S(1)} %constant_dynamic-slice_fusion.4, bf16[256,1024]{1,0:T(8,128)(2,1)S(1)} %constant_dynamic-slice_fusion.5), kind=kOutput, calls=%fused_computation.2.clone.1 | convolution fusion | flops 1629487104 | bytes 8388608 | tf_op jit(solution)/shard_map/while/body/eval_jaxpr/dot_general | solution.py:45
  511.8 5.6 maximum_add_fusion.5
  522.7 12.8 %convolution_bitcast_fusion.2 = f32[512,3072]{1,0:T(8,128)S(1)} fusion(bf16[512,512]{1,0:T(8,128)(2,1)} %get-tuple-element.451, bf16[256,1024]{1,0:T(8,128)(2,1)} %copy.23, bf16[256,1024]{1,0:T(8,128)(2,1)S(1)} %constant_dynamic-slice_fusion.4, bf16[256,1024]{1,0:T(8,128)(2,1)S(1)} %constant_dynamic-slice_fusion.5), kind=kOutput, calls=%fused_computation.2.clone.1 | convolution fusion | flops 1629487104 | bytes 8388608 | tf_op jit(solution)/shard_map/while/body/eval_jaxpr/dot_general | solution.py:45
  542.4 5.6 maximum_add_fusion.5
  553.4 12.8 %convolution_bitcast_fusion.2 = f32[512,3072]{1,0:T(8,128)S(1)} fusion(bf16[512,512]{1,0:T(8,128)(2,1)} %get-tuple-element.451, bf16[256,1024]{1,0:T(8,128)(2,1)} %copy.23, bf16[256,1024]{1,0:T(8,128)(2,1)S(1)} %constant_dynamic-slice_fusion.4, bf16[256,1024]{1,0:T(8,128)(2,1)S(1)} %constant_dynamic-slice_fusion.5), kind=kOutput, calls=%fused_computation.2.clone.1 | convolution fusion | flops 1629487104 | bytes 8388608 | tf_op jit(solution)/shard_map/while/body/eval_jaxpr/dot_general | solution.py:45
  584.0 12.8 %convolution_bitcast_fusion.2 = f32[512,3072]{1,0:T(8,128)S(1)} fusion(bf16[512,512]{1,0:T(8,128)(2,1)} %get-tuple-element.451, bf16[256,1024]{1,0:T(8,128)(2,1)} %copy.23, bf16[256,1024]{1,0:T(8,128)(2,1)S(1)} %constant_dynamic-slice_fusion.4, bf16[256,1024]{1,0:T(8,128)(2,1)S(1)} %constant_dynamic-slice_fusion.5), kind=kOutput, calls=%fused_computation.2.clone.1 | convolution fusion | flops 1629487104 | bytes 8388608 | tf_op jit(solution)/shard_map/while/body/eval_jaxpr/dot_general | solution.py:45
  614.7 12.8 %convolution_bitcast_fusion.2 = f32[512,3072]{1,0:T(8,128)S(1)} fusion(bf16[512,512]{1,0:T(8,128)(2,1)} %get-tuple-element.451, bf16[256,1024]{1,0:T(8,128)(2,1)} %copy.23, bf16[256,1024]{1,0:T(8,128)(2,1)S(1)} %constant_dynamic-slice_fusion.4, bf16[256,1024]{1,0:T(8,128)(2,1)S(1)} %constant_dynamic-slice_fusion.5), kind=kOutput, calls=%fused_computation.2.clone.1 | convolution fusion | flops 1629487104 | bytes 8388608 | tf_op jit(solution)/shard_map/while/body/eval_jaxpr/dot_general | solution.py:45
  640.0 6.3 fusion.21
  652.6 5.8 fusion.17
  659.2 85.7 %psum.14 = f32[]{:T(128)} all-reduce(f32[]{:T(128)} %multiply_reduce_fusion.3), channel_id=1, replica_groups=mesh['ctx'=16,'ch'=8] {'ctx','ch'}, use_global_device_ids=true, to_apply=%region_3.4 | all-reduce | flops 1 | bytes 8 | tf_op jit(solution)/shard_map/psum | solution.py:143
  750.9 54.9 %psum.15 = f32[3,1024]{1,0:T(4,128)} all-reduce(f32[3,1024]{1,0:T(4,128)S(1)} %pad_maximum_fusion.2), channel_id=1, replica_groups=mesh['ctx'=16,'ch'=8] {'ctx'}, use_global_device_ids=true, to_apply=%region_7.8 | all-reduce | flops 3072 | bytes 24576 | tf_op jit(solution)/shard_map/psum | solution.py:141
  (211 shorter events, 252.4 us)
Async XLA Ops:
  7.2 169.3 %all-gather.2.cloned.1.call-start = ((), (), s32[]{:S(2)}) async-start(), calls=%async_computation.1 | async-start | bytes 8912896 | tf_op jit(solution)/shard_map/all_gather | solution.py:63
  7.9 2.1 collective-permute-start.1
  11.3 3.0 copy-start.2
  11.3 3.0 copy-start.6
  18.6 155.9 %all-to-all-start = ((bf16[16,256,1024]{2,1,0:T(8,128)(2,1)}), bf16[16,256,1024]{2,1,0:T(8,128)(2,1)}, u32[]{:S(2)}, u32[]{:S(2)}) async-start(bf16[16,256,1024]{2,1,0:T(8,128)(2,1)} %stack.10), calls=%async_computation | async-start | bytes 16777216 | tf_op jit(solution)/shard_map/all_to_all | solution.py:13
  27.0 6.9 copy-start.7
  27.0 6.9 copy-start.8
  27.0 6.9 copy-start.9
  32.4 0.7 copy-start.5
  183.3 27.5 %collective-permute-start = (bf16[256,1024]{1,0:T(8,128)(2,1)}, bf16[256,1024]{1,0:T(8,128)(2,1)}, u32[]{:S(2)}, u32[]{:S(2)}) collective-permute-start(bf16[256,1024]{1,0:T(8,128)(2,1)} %copy.23), channel_id=1, source_target_pairs={{8,0},{16,8},{24,16},{32,24},{40,32},{48,40},{56,48},{64,56},{72,6... | collective-permute-start | bytes 1572872 | tf_op jit(solution)/shard_map/while/body/eval_jaxpr/ppermute | solution.py:20
  212.7 28.8 %collective-permute-start = (bf16[256,1024]{1,0:T(8,128)(2,1)}, bf16[256,1024]{1,0:T(8,128)(2,1)}, u32[]{:S(2)}, u32[]{:S(2)}) collective-permute-start(bf16[256,1024]{1,0:T(8,128)(2,1)} %copy.23), channel_id=1, source_target_pairs={{8,0},{16,8},{24,16},{32,24},{40,32},{48,40},{56,48},{64,56},{72,6... | collective-permute-start | bytes 1572872 | tf_op jit(solution)/shard_map/while/body/eval_jaxpr/ppermute | solution.py:20
  243.3 28.8 %collective-permute-start = (bf16[256,1024]{1,0:T(8,128)(2,1)}, bf16[256,1024]{1,0:T(8,128)(2,1)}, u32[]{:S(2)}, u32[]{:S(2)}) collective-permute-start(bf16[256,1024]{1,0:T(8,128)(2,1)} %copy.23), channel_id=1, source_target_pairs={{8,0},{16,8},{24,16},{32,24},{40,32},{48,40},{56,48},{64,56},{72,6... | collective-permute-start | bytes 1572872 | tf_op jit(solution)/shard_map/while/body/eval_jaxpr/ppermute | solution.py:20
  274.0 28.8 %collective-permute-start = (bf16[256,1024]{1,0:T(8,128)(2,1)}, bf16[256,1024]{1,0:T(8,128)(2,1)}, u32[]{:S(2)}, u32[]{:S(2)}) collective-permute-start(bf16[256,1024]{1,0:T(8,128)(2,1)} %copy.23), channel_id=1, source_target_pairs={{8,0},{16,8},{24,16},{32,24},{40,32},{48,40},{56,48},{64,56},{72,6... | collective-permute-start | bytes 1572872 | tf_op jit(solution)/shard_map/while/body/eval_jaxpr/ppermute | solution.py:20
  304.6 28.8 %collective-permute-start = (bf16[256,1024]{1,0:T(8,128)(2,1)}, bf16[256,1024]{1,0:T(8,128)(2,1)}, u32[]{:S(2)}, u32[]{:S(2)}) collective-permute-start(bf16[256,1024]{1,0:T(8,128)(2,1)} %copy.23), channel_id=1, source_target_pairs={{8,0},{16,8},{24,16},{32,24},{40,32},{48,40},{56,48},{64,56},{72,6... | collective-permute-start | bytes 1572872 | tf_op jit(solution)/shard_map/while/body/eval_jaxpr/ppermute | solution.py:20
  335.3 28.8 %collective-permute-start = (bf16[256,1024]{1,0:T(8,128)(2,1)}, bf16[256,1024]{1,0:T(8,128)(2,1)}, u32[]{:S(2)}, u32[]{:S(2)}) collective-permute-start(bf16[256,1024]{1,0:T(8,128)(2,1)} %copy.23), channel_id=1, source_target_pairs={{8,0},{16,8},{24,16},{32,24},{40,32},{48,40},{56,48},{64,56},{72,6... | collective-permute-start | bytes 1572872 | tf_op jit(solution)/shard_map/while/body/eval_jaxpr/ppermute | solution.py:20
  365.9 28.8 %collective-permute-start = (bf16[256,1024]{1,0:T(8,128)(2,1)}, bf16[256,1024]{1,0:T(8,128)(2,1)}, u32[]{:S(2)}, u32[]{:S(2)}) collective-permute-start(bf16[256,1024]{1,0:T(8,128)(2,1)} %copy.23), channel_id=1, source_target_pairs={{8,0},{16,8},{24,16},{32,24},{40,32},{48,40},{56,48},{64,56},{72,6... | collective-permute-start | bytes 1572872 | tf_op jit(solution)/shard_map/while/body/eval_jaxpr/ppermute | solution.py:20
  396.6 28.8 %collective-permute-start = (bf16[256,1024]{1,0:T(8,128)(2,1)}, bf16[256,1024]{1,0:T(8,128)(2,1)}, u32[]{:S(2)}, u32[]{:S(2)}) collective-permute-start(bf16[256,1024]{1,0:T(8,128)(2,1)} %copy.23), channel_id=1, source_target_pairs={{8,0},{16,8},{24,16},{32,24},{40,32},{48,40},{56,48},{64,56},{72,6... | collective-permute-start | bytes 1572872 | tf_op jit(solution)/shard_map/while/body/eval_jaxpr/ppermute | solution.py:20
  427.3 28.8 %collective-permute-start = (bf16[256,1024]{1,0:T(8,128)(2,1)}, bf16[256,1024]{1,0:T(8,128)(2,1)}, u32[]{:S(2)}, u32[]{:S(2)}) collective-permute-start(bf16[256,1024]{1,0:T(8,128)(2,1)} %copy.23), channel_id=1, source_target_pairs={{8,0},{16,8},{24,16},{32,24},{40,32},{48,40},{56,48},{64,56},{72,6... | collective-permute-start | bytes 1572872 | tf_op jit(solution)/shard_map/while/body/eval_jaxpr/ppermute | solution.py:20
  457.9 28.8 %collective-permute-start = (bf16[256,1024]{1,0:T(8,128)(2,1)}, bf16[256,1024]{1,0:T(8,128)(2,1)}, u32[]{:S(2)}, u32[]{:S(2)}) collective-permute-start(bf16[256,1024]{1,0:T(8,128)(2,1)} %copy.23), channel_id=1, source_target_pairs={{8,0},{16,8},{24,16},{32,24},{40,32},{48,40},{56,48},{64,56},{72,6... | collective-permute-start | bytes 1572872 | tf_op jit(solution)/shard_map/while/body/eval_jaxpr/ppermute | solution.py:20
  488.6 28.8 %collective-permute-start = (bf16[256,1024]{1,0:T(8,128)(2,1)}, bf16[256,1024]{1,0:T(8,128)(2,1)}, u32[]{:S(2)}, u32[]{:S(2)}) collective-permute-start(bf16[256,1024]{1,0:T(8,128)(2,1)} %copy.23), channel_id=1, source_target_pairs={{8,0},{16,8},{24,16},{32,24},{40,32},{48,40},{56,48},{64,56},{72,6... | collective-permute-start | bytes 1572872 | tf_op jit(solution)/shard_map/while/body/eval_jaxpr/ppermute | solution.py:20
  519.2 28.8 %collective-permute-start = (bf16[256,1024]{1,0:T(8,128)(2,1)}, bf16[256,1024]{1,0:T(8,128)(2,1)}, u32[]{:S(2)}, u32[]{:S(2)}) collective-permute-start(bf16[256,1024]{1,0:T(8,128)(2,1)} %copy.23), channel_id=1, source_target_pairs={{8,0},{16,8},{24,16},{32,24},{40,32},{48,40},{56,48},{64,56},{72,6... | collective-permute-start | bytes 1572872 | tf_op jit(solution)/shard_map/while/body/eval_jaxpr/ppermute | solution.py:20
  549.9 28.8 %collective-permute-start = (bf16[256,1024]{1,0:T(8,128)(2,1)}, bf16[256,1024]{1,0:T(8,128)(2,1)}, u32[]{:S(2)}, u32[]{:S(2)}) collective-permute-start(bf16[256,1024]{1,0:T(8,128)(2,1)} %copy.23), channel_id=1, source_target_pairs={{8,0},{16,8},{24,16},{32,24},{40,32},{48,40},{56,48},{64,56},{72,6... | collective-permute-start | bytes 1572872 | tf_op jit(solution)/shard_map/while/body/eval_jaxpr/ppermute | solution.py:20
  580.5 28.8 %collective-permute-start = (bf16[256,1024]{1,0:T(8,128)(2,1)}, bf16[256,1024]{1,0:T(8,128)(2,1)}, u32[]{:S(2)}, u32[]{:S(2)}) collective-permute-start(bf16[256,1024]{1,0:T(8,128)(2,1)} %copy.23), channel_id=1, source_target_pairs={{8,0},{16,8},{24,16},{32,24},{40,32},{48,40},{56,48},{64,56},{72,6... | collective-permute-start | bytes 1572872 | tf_op jit(solution)/shard_map/while/body/eval_jaxpr/ppermute | solution.py:20
  611.2 28.8 %collective-permute-start = (bf16[256,1024]{1,0:T(8,128)(2,1)}, bf16[256,1024]{1,0:T(8,128)(2,1)}, u32[]{:S(2)}, u32[]{:S(2)}) collective-permute-start(bf16[256,1024]{1,0:T(8,128)(2,1)} %copy.23), channel_id=1, source_target_pairs={{8,0},{16,8},{24,16},{32,24},{40,32},{48,40},{56,48},{64,56},{72,6... | collective-permute-start | bytes 1572872 | tf_op jit(solution)/shard_map/while/body/eval_jaxpr/ppermute | solution.py:20
  649.0 1.6 copy-start
  649.0 2.2 copy-start.1
  652.6 93.0 %copy-start.3 = (f32[258,1024]{1,0:T(8,128)S(1)}, f32[258,1024]{1,0:T(8,128)}, u32[]{:S(2)}) copy-start(f32[258,1024]{1,0:T(8,128)} %copy-done.2) | copy-start | bytes 3170308
  748.6 1.0 copy-start.4
  749.6 56.3 %collective-permute-start.2 = (f32[2,1024]{1,0:T(2,128)S(1)}, f32[2,1024]{1,0:T(2,128)S(1)}, u32[]{:S(2)}, u32[]{:S(2)}) collective-permute-start(f32[2,1024]{1,0:T(2,128)S(1)} %slice.191), channel_id=1, source_target_pairs={{8,0},{16,8},{24,16},{32,24},{40,32},{48,40},{56,48},{64,56},{72,6... | collective-permute-start | bytes 24584 | tf_op jit(solution)/shard_map/ppermute | solution.py:20
Sparse Core Ops, SparseCore 0:
  14.4 149.0 all-gather.1
